TPU v7x, 128 devices: a whole 4x4x4 slice. The times are simulated.
128 devices in a mesh: inst: 32 (over z, y, x_hi), head: 4 (over x_lo, core).
Axes of the slice: x: 4 (x_hi: 2, x_lo: 2; x = x_hi * 2 + x_lo), y: 4, z: 4, core: 2. Of those that a mesh axis runs over, the one named last changes fastest.
Arguments:
- queries: bfloat16 [8192, 32, 128], P('inst', 'head'), may hold values from -120 to 120
- keys: bfloat16 [8192, 4, 128], P('inst', 'head'), may hold values from -6 to 6
- values: bfloat16 [8192, 4, 128], P('inst', 'head'), may hold values from -6 to 6
- lengths: int32 [4], replicated, may hold values from 1 to 5120, 8192 in all
- prior_kv: bfloat16 [16384, 4, 256], P('inst', 'head'), may hold values from -6 to 6
- routes: int32 [1024, 1], P('inst'), may hold values from 0 to 31; in each aligned block of 32 rows (0 to 31, 32 to 63, ...) at most 2 rows name the same one
- out_weight: bfloat16 [4096, 4096], P('head'), may hold values from -0.09375 to 0.09375
Outputs:
- projected: bfloat16 [8192, 4096], P(('inst', 'head'))
- migrated: bfloat16 [2048, 16, 4, 256], P('inst', None, 'head')
Inputs may be any that keep to these rules, and one draw needn't show every extreme that they name: The 4 lengths sum to 8192; the longest is exactly 5120. `routes`: among the 32 blocks of one source shard no target is named more than 2 times, and some source names some target exactly 2 times.
All inputs are finite; a program needn't handle non-finite values.
Results may differ from a plain program's by a relative error of at most 0.013.
Values may be sent and summed in bfloat16 or wider, within the bound.
A program may use at most 192 MiB of HBM per device.

v0:
```python
import math

import jax
import jax.numpy as jnp
from jax import lax
from jax.sharding import PartitionSpec as P

BLOCK = 16


def doc_index(positions, doc_ends):
    return jnp.sum((positions[:, None] >= doc_ends[None, :]).astype(jnp.int32), axis=1)


def shards(queries, keys, values, lengths, prior_kv, routes, out_weight):
    tok_rows, heads_local, head_size = queries.shape
    kv_local = keys.shape[1]
    group_size = heads_local // kv_local
    inst_count = lax.axis_size("inst")
    my_index = lax.axis_index("inst")
    query_first = my_index * tok_rows
    doc_ends = jnp.cumsum(lengths)
    query_pos = query_first + jnp.arange(tok_rows, dtype=jnp.int32)
    query_doc = doc_index(query_pos, doc_ends)
    query_grouped = queries.reshape(tok_rows, kv_local, group_size, head_size)
    score_scale = 1.0 / math.sqrt(head_size)
    key_piece = lax.all_gather(keys, "inst", axis=0, tiled=True)
    value_piece = lax.all_gather(values, "inst", axis=0, tiled=True)
    piece_rows = key_piece.shape[0]
    key_pos = jnp.arange(piece_rows, dtype=jnp.int32)
    key_doc = doc_index(key_pos, doc_ends)
    allowed = (
        (key_pos[None, :] <= query_pos[:, None])
        & (key_doc[None, :] == query_doc[:, None])
        & (key_pos[None, :] >= 0)
    )
    scores = (
        jnp.einsum("qcgd,kcd->cgqk", query_grouped, key_piece, preferred_element_type=jnp.float32)
        * score_scale
    )
    scores = jnp.where(allowed[None, None], scores, -1e30)
    running = jnp.full((kv_local, group_size, tok_rows), -1e30, jnp.float32)
    top_score = jnp.maximum(running, jnp.max(scores, axis=-1))
    weights = jnp.where(allowed[None, None], jnp.exp(scores - top_score[..., None]), 0.0)
    totals = jnp.sum(weights, axis=-1)
    update = jnp.einsum(
        "cgqk,kcd->cgqd",
        weights.astype(jnp.bfloat16),
        value_piece,
        preferred_element_type=jnp.float32,
    )
    accumulated = update
    top_score, totals, accumulated = (top_score, totals, accumulated)
    blended = accumulated / totals[..., None]
    attended = (
        jnp.transpose(blended, (2, 0, 1, 3))
        .reshape(tok_rows, heads_local * head_size)
        .astype(jnp.bfloat16)
    )
    projected = lax.psum_scatter(
        jnp.dot(attended, out_weight, preferred_element_type=jnp.float32).astype(jnp.bfloat16),
        "head",
        scatter_dimension=0,
        tiled=True,
    )
    block_count = prior_kv.shape[0] // BLOCK
    most_slots = max(2, (2 * block_count + inst_count - 1) // inst_count)
    flattened = prior_kv.reshape(block_count, -1)
    target = routes[:, 0]
    onehot = (target[:, None] == jnp.arange(inst_count, dtype=jnp.int32)[None, :]).astype(jnp.int32)
    order_rank = jnp.sum((jnp.cumsum(onehot, axis=0) - onehot) * onehot, axis=1)
    slot_hit = (jnp.arange(most_slots, dtype=jnp.int32)[None, :] == order_rank[:, None]).astype(
        jnp.int32
    )
    chooser = (onehot[:, :, None] * slot_hit[:, None, :]).astype(jnp.bfloat16)
    outgoing = jnp.einsum(
        "jdk,jx->dkx", chooser, flattened, preferred_element_type=jnp.float32
    ).astype(jnp.bfloat16)
    outgoing = outgoing.reshape(inst_count, most_slots, BLOCK, kv_local, 2 * head_size)
    arrived = lax.all_to_all(outgoing, "inst", split_axis=0, concat_axis=0, tiled=True)
    migrated = arrived.reshape(inst_count * most_slots, BLOCK, kv_local, 2 * head_size)
    return (projected, migrated)


def solution(mesh):
    placed = (
        P("inst", "head", None),
        P("inst", "head", None),
        P("inst", "head", None),
        P(),
        P("inst", "head", None),
        P("inst", None),
        P("head", None),
    )
    return jax.shard_map(
        shards,
        mesh=mesh,
        in_specs=placed,
        out_specs=(P(("inst", "head"), None), P("inst", None, "head", None)),
        check_vma=False,
    )
```

profile of v0, /device:TPU:97, one launch (start us, length us, event | category | flops | bytes accessed | tf_op | source)
XLA Modules:
  0.0 223.6 jit_solution(4031433076607116200)
XLA Ops:
  7.2 0.0 copy-start
  7.2 0.0 all-gather.3.cloned.1.call-start
  7.2 0.7 all-gather.3.cloned.1.call-update
  7.9 0.0 all-gather.5.cloned.1.call-start
  8.0 1.6 copy.21
  9.5 0.0 all-gather.5.cloned.1.call-update
  9.6 0.0 reduce-scatter.2.cloned.1.call-start
  9.6 0.8 reduce-window.8
  10.5 0.2 convert_reduce_fusion
  10.6 0.1 convert_reduce_fusion.1
  10.7 3.7 %fusion.7 = pred[256,8192]{0,1:T(8,128)(4,1)S(1)} fusion(s32[256]{0:T(256)S(1)} %convert_reduce_fusion.1, s32[256]{0:T(256)S(1)} %iota_add_fusion, s32[8192]{0:T(1024)S(1)} %convert_reduce_fusion), kind=kLoop, calls=%fused_computation.9 | loop fusion | flops 6291456 | bytes 2131968 | tf_op jit(solution)/shard_map/and | solution.py:33
  14.4 66.7 %all-gather.3.cloned.1.call-done = bf16[8192,1,128]{2,0,1:T(8,128)(2,1)} async-done(((bf16[256,1,128]{2,0,1:T(8,128)(2,1)}), bf16[8192,1,128]{2,0,1:T(8,128)(2,1)}) %all-gather.3.cloned.1.call-update) | async-done | bytes 2097168 | tf_op jit(solution)/shard_map/all_gather | solution.py:27
  81.2 0.0 copy-done
  81.2 25.0 %fusion = (f32[8,256]{1,0:T(8,128)S(1)}, f32[8192,256,8]{1,0,2:T(8,128)}) fusion(pred[256,8192]{0,1:T(8,128)(4,1)S(1)} %fusion.7, bf16[256,8,128]{2,1,0:T(8,128)(2,1)S(1)} %copy-done, bf16[8192,1,128]{2,0,1:T(8,128)(2,1)} %all-gather.3.cloned.1.call-done), kind=kOutput, calls=%fused_computation.2 | convolution fusion | flops 4345296896 | bytes 71835648 | tf_op jit(solution)/shard_map/qcgd,kcd->cgqk/dot_general | solution.py:38
  106.2 21.9 %fusion.1 = f32[8,256]{1,0:T(8,128)S(1)} fusion(f32[8192,256,8]{1,0,2:T(8,128)} %get-tuple-element.7, f32[8,256]{1,0:T(8,128)S(1)} %broadcast_maximum_fusion, pred[256,8192]{0,1:T(8,128)(4,1)S(1)} %fusion.7), kind=kLoop, calls=%fused_computation.3 | loop fusion | flops 83884032 | bytes 69222400 | tf_op jit(solution)/shard_map/reduce_sum | solution.py:45
  128.0 0.0 copy-start.2
  128.1 0.0 copy-start.1
  128.1 23.1 %all-gather.5.cloned.1.call-done = bf16[8192,1,128]{0,2,1:T(8,128)(2,1)} async-done(((bf16[256,1,128]{0,2,1:T(8,128)(2,1)}), bf16[8192,1,128]{0,2,1:T(8,128)(2,1)}) %all-gather.5.cloned.1.call-update) | async-done | bytes 2097168 | tf_op jit(solution)/shard_map/all_gather | solution.py:28
  151.2 24.7 %divide_convert_fusion = bf16[8,256,128]{1,2,0:T(8,128)(2,1)S(1)} fusion(f32[8192,256,8]{1,0,2:T(8,128)} %get-tuple-element.7, f32[8,256]{1,0:T(8,128)S(1)} %broadcast_maximum_fusion, pred[256,8192]{0,1:T(8,128)(4,1)S(1)} %fusion.7, bf16[8192,1,128]{0,2,1:T(8,128)(2,1)} %all-gather.5.cloned.1.call-done, f32[8,256]{1,0:T(8,128)S(1)} %fusion.1), kind=kOutput, calls=%fused_computation.15 | convolution fusion | flops 4379377664 | bytes 71843840 | tf_op jit(solution)/shard_map/cgqk,kcd->cgqd/dot_general | solution.py:46
  175.9 7.1 %convolution_convert_fusion = bf16[256,4096]{1,0:T(8,128)(2,1)} fusion(bf16[256,1024]{0,1:T(8,128)(2,1)S(1)} %bitcast.59, bf16[1024,4096]{1,0:T(8,128)(2,1)} %param.13), kind=kOutput, calls=%fused_computation.10 | convolution fusion | flops 2148532224 | bytes 11010048 | tf_op jit(solution)/shard_map/dot_general | solution.py:61
  183.1 0.0 reduce-scatter.2.cloned.1.call-update
  183.1 0.0 copy-done.2
  183.1 0.1 fusion.18
  183.2 0.1 reduce_window_sum.18
  183.2 0.1 copy.23
  183.3 0.0 copy-done.1
  183.3 0.1 reshape.178
  183.4 0.2 select_reduce_fusion
  183.6 0.3 convolution_convert_fusion.1
  183.9 0.1 copy.27
  184.0 0.1 copy.24
  184.1 22.4 %all_to_all.5 = bf16[32,2,16,1,256]{4,2,1,3,0:T(8,128)(2,1)S(1)} all-to-all(bf16[32,2,16,1,256]{4,2,1,3,0:T(8,128)(2,1)S(1)} %copy.24), channel_id=1, replica_groups=mesh['inst'=32,'head'=4] {'inst'}, dimensions={0} | all-to-all | bytes 1048576 | tf_op jit(solution)/shard_map/all_to_all | solution.py:80
  206.5 9.8 %reduce-scatter.2.cloned.1.call-done = bf16[64,4096]{1,0:T(8,128)(2,1)} async-done(((bf16[256,4096]{1,0:T(8,128)(2,1)}), bf16[64,4096]{1,0:T(8,128)(2,1)}) %reduce-scatter.2.cloned.1.call-update) | async-done | bytes 524304 | tf_op jit(solution)/shard_map/reduce_scatter | solution.py:60
  216.3 0.8 copy.33
  (3 shorter events, 0.0 us)
Async XLA Ops:
  7.2 74.0 %copy-start = (bf16[256,8,128]{2,1,0:T(8,128)(2,1)S(1)}, bf16[256,8,128]{2,1,0:T(8,128)(2,1)}, u32[]{:S(2)}) copy-start(bf16[256,8,128]{2,1,0:T(8,128)(2,1)} %param.7) | copy-start | bytes 1572868
  7.2 74.0 %all-gather.3.cloned.1.call-start = ((), (), s32[]{:S(2)}) async-start(), calls=%async_computation.2 | async-start | bytes 2162688 | tf_op jit(solution)/shard_map/all_gather | solution.py:27
  7.9 143.3 %all-gather.5.cloned.1.call-start = ((), (), s32[]{:S(2)}) async-start(), calls=%async_computation.3 | async-start | bytes 2162688 | tf_op jit(solution)/shard_map/all_gather | solution.py:28
  9.6 206.7 %reduce-scatter.2.cloned.1.call-start = ((), (), s32[]{:S(2)}) async-start(), calls=%async_computation.4 | async-start | bytes 2621440 | tf_op jit(solution)/shard_map/reduce_scatter | solution.py:60
  128.0 55.0 %copy-start.2 = (s32[32,1]{0,1:T(1,128)S(1)}, s32[32,1]{0,1:T(1,128)}, u32[]{:S(2)}) copy-start(s32[32,1]{0,1:T(1,128)} %param.12) | copy-start | bytes 388
  128.1 55.2 %copy-start.1 = (bf16[512,1,256]{2,0,1:T(8,128)(2,1)S(1)}, bf16[512,1,256]{2,0,1:T(8,128)(2,1)}, u32[]{:S(2)}) copy-start(bf16[512,1,256]{2,0,1:T(8,128)(2,1)} %param.11) | copy-start | bytes 786436
Sparse Core Ops, SparseCore 0:
  11.1 70.0 all-gather.2
  84.5 66.6 all-gather.4
  183.2 33.0 reduce-scatter.1
where the time goes:
time: 226 us; the launch traced here: 224 us
  waiting for transfers between devices  100 us (44%)
  matrix products  57.1 us (25%)
  other arithmetic  27 us (12%)
  blocking collectives  22.4 us (10%)
  between operations  13.9 us (6%)
  local copies, waits for them, and re-layouts  2.75 us (1%)
    all_gather x1, waiting for transfers between devices, shards(): key_piece = lax.all_gather(keys, 'inst', axis=0, tiled=True)  66.7 us
    dot_general x1, matrix products, shards(): jnp.einsum('qcgd,kcd->cgqk', query_grouped, key_piece, preferred_element_...  25 us
    dot_general x1, matrix products, shards(): jnp.einsum('cgqk,kcd->cgqd', weights.astype(jnp.bfloat16), value_piece, p...  24.7 us
    all_gather x1, waiting for transfers between devices, shards(): value_piece = lax.all_gather(values, 'inst', axis=0, tiled=True)  23.1 us
    all_to_all x1, blocking collectives, shards(): lax.all_to_all(outgoing, 'inst', split_axis=0, concat_axis=0, tiled=True)  22.4 us
    reduce_sum x1, other arithmetic, shards(): totals = jnp.sum(weights, axis=-1)  21.9 us
    reduce_scatter x1, waiting for transfers between devices, shards(): lax.psum_scatter(jnp.dot(attended, out_weight, preferred_element_type=jnp...  9.76 us
    dot_general x1, matrix products, shards(): jnp.dot(attended, out_weight, preferred_element_type=jnp.float32)  7.12 us
  transfers between devices with their start and end apart: 3, of which 3 were waited for; matrix products, arithmetic and copies ran while one was open for 24% of the time, Pallas kernels for 0%

commit v1 on v0

v1 whole, which is shorter than its diff:
```python
import functools
import math

import jax
import jax.numpy as jnp
from jax import lax
from jax.experimental import pallas as pl
from jax.experimental.pallas import tpu as pltpu
from jax.sharding import PartitionSpec as P

MESH = pl.DeviceIdType.MESH
F32, BF16 = jnp.float32, jnp.bfloat16
BLOCK = 16
TOK = 256
HEADS = 8
HD = 128
N_INST = 32
WINDOW = 20
GRP = 4
PAD = 4
PARTS = ((0, 96), (96, 48), (144, 112))
QROWS = 512
TILE = 256
CHUNKS = 4
CW = 1024
BIG = float(2 ** 30)
SCALE = math.log2(math.e) / math.sqrt(HD)


def doc_of(positions, ends):
    doc = jnp.zeros(positions.shape, jnp.int32)
    for e in ends:
        doc = doc + (positions >= e).astype(jnp.int32)
    return doc


def kernel(lengths, q_hbm, k_ref, v_ref, prior_hbm, rcol, rrow, w_hbm,
           out_ref, mig_ref,
           kv, feat, qraw, qf, qx, acc, mx, prior, outgoing, wbuf, att,
           keep, s1_out, s1_in, x_out, x_in, s2_out, s2_in,
           loc, ssem, rsem, msem, mrsem, rs_s, rs_r):
    me = lax.axis_index("inst")
    hd = lax.axis_index("head")
    z, r = me // 8, lax.rem(me, 8)
    y, h = r // 2, lax.rem(r, 2)
    xl, c = hd // 2, lax.rem(hd, 2)
    sib = (me, 2 * xl + 1 - c)
    across = (me, 2 * (1 - xl) + c)

    q_copy = pltpu.make_async_copy(q_hbm, qraw, loc.at[0])
    p_copy = pltpu.make_async_copy(prior_hbm, prior, loc.at[1])
    w_copy = pltpu.make_async_copy(w_hbm, wbuf, loc.at[2])
    q_copy.start()
    p_copy.start()
    w_copy.start()

    barrier = pltpu.get_barrier_semaphore()

    def greet(d, carry):
        pl.semaphore_signal(barrier, inc=1, device_id=(lax.rem(me + d, N_INST), hd), device_id_type=MESH)
        return carry

    lax.fori_loop(1, N_INST, greet, 0)
    pl.semaphore_signal(barrier, inc=1, device_id=sib, device_id_type=MESH)
    pl.semaphore_signal(barrier, inc=1, device_id=across, device_id_type=MESH)

    own = pl.multiple_of((me + PAD) * TOK, TOK)
    kv[pl.ds(own, TOK), :HD] = k_ref[...]
    kv[pl.ds(own, TOK), HD:] = v_ref[...]
    pl.semaphore_wait(barrier, N_INST + 1)

    def piece(part, blk):
        first, rows = PARTS[part]
        return kv.at[pl.ds(pl.multiple_of((blk + PAD) * TOK + first, 16), rows), :]

    def send(part, blk, target, slot):
        return pltpu.make_async_remote_copy(
            src_ref=piece(part, blk), dst_ref=piece(part, blk),
            send_sem=ssem.at[part, slot], recv_sem=rsem.at[part, blk],
            device_id=(target, hd), device_id_type=MESH)

    def arrive(part, blk):
        send(part, blk, me, 0).wait_recv()

    def z_first(part, act):
        def one(dz, carry):
            @pl.when((z + dz < 4) & ((dz < 3) | (r >= 4)))
            def _():
                act(send(part, me, me + 8 * dz, dz - 1))
            return carry
        lax.fori_loop(1, 4, one, 0)

    def p0_h(act):
        act(send(0, me, z * 8 + y * 2 + 1 - h, 0))

    def p0_y(act):
        def one(n, carry):
            y2 = lax.rem(y + 1 + n // 2, 4)
            act(send(0, z * 8 + y * 2 + lax.rem(n, 2), z * 8 + y2 * 2 + h, 1 + n))
            return carry
        lax.fori_loop(0, 6, one, 0)

    def needs(dst, src):
        return (dst - src >= 1) & (dst - src <= WINDOW)

    def p0_z(act):
        def one(n, carry):
            dz, src = 1 + n // 8, z * 8 + 7 - lax.rem(n, 8)
            dst = me + 8 * dz
            @pl.when((z + dz < 4) & needs(dst, src))
            def _():
                act(send(0, src, dst, 7 + n))
            return carry
        lax.fori_loop(0, 24, one, 0)

    def p1_h(act):
        def one(dz, carry):
            @pl.when((z >= dz) & ((dz < 3) | (r >= 4)))
            def _():
                act(send(1, me - 8 * dz, z * 8 + y * 2 + 1 - h, 3 + dz))
            return carry
        lax.fori_loop(0, 4, one, 0)

    def p1_y(act):
        def one(n, carry):
            dz = n // 6
            y2 = lax.rem(y + 1 + lax.rem(n, 6) // 2, 4)
            src = (z - dz) * 8 + y * 2 + lax.rem(n, 2)
            dst = z * 8 + y2 * 2 + h
            @pl.when((z >= dz) & needs(dst, src))
            def _():
                act(send(1, src, dst, 7 + n))
            return carry
        lax.fori_loop(0, 24, one, 0)

    def y_wants(dz, src_r, src_y, y2):
        return (((dz == 0) & (y2 > src_y)) | (dz == 1)
                | ((dz == 2) & (src_r >= 2 * y2 - 4)) | ((dz == 3) & (src_r >= 2 * y2 + 4)))

    def p2_y(act):
        def one(n, carry):
            dz = n // 3
            y2 = lax.rem(y + 1 + lax.rem(n, 3), 4)
            @pl.when((z >= dz) & y_wants(dz, r, y, y2))
            def _():
                act(send(2, me - 8 * dz, z * 8 + y2 * 2 + h, 3 + n))
            return carry
        lax.fori_loop(0, 12, one, 0)

    def p2_h(act):
        def one(n, carry):
            dz, y1 = n // 4, 3 - lax.rem(n, 4)
            src = (z - dz) * 8 + y1 * 2 + h
            dst = z * 8 + y * 2 + 1 - h
            @pl.when((z >= dz) & needs(dst, src))
            def _():
                act(send(2, src, dst, 15 + n))
            return carry
        lax.fori_loop(0, 16, one, 0)

    start = lambda copy: copy.start()
    done = lambda copy: copy.wait_send()

    p0_h(start)
    z_first(1, start)
    z_first(2, start)

    ends = []
    total = jnp.int32(0)
    for i in range(4):
        total = total + lengths[i]
        ends.append(total)
    kv[: PAD * TOK, :] = jnp.zeros((PAD * TOK, 2 * HD), BF16)

    def key_feature(b, carry):
        pos = (b - PAD) * TOK + lax.broadcasted_iota(jnp.int32, (TOK, HD), 0)
        lane = lax.broadcasted_iota(jnp.int32, (TOK, HD), 1)
        doc = jnp.where(pos < 0, 4, doc_of(pos, ends))
        feat[pl.ds(pl.multiple_of(b * TOK, TOK), TOK), :] = jnp.where(doc == lane, 1.0, 0.0).astype(BF16)
        return carry

    lax.fori_loop(0, N_INST + PAD, key_feature, 0)

    q_copy.wait()

    def widen(t, carry):
        rows = pl.ds(pl.multiple_of(t * TILE, TILE), TILE)
        qf[rows, :] = qraw[rows, :].astype(F32)
        return carry

    lax.fori_loop(0, 8, widen, 0)
    for quarter in range(4):
        pos = me * TOK + quarter * 64 + lax.broadcasted_iota(jnp.int32, (64, HD), 0)
        lane = lax.broadcasted_iota(jnp.int32, (64, HD), 1)
        doc = doc_of(pos, ends)
        mask = jnp.where((lane < 5) & (lane != doc), -BIG, 0.0).astype(BF16)
        for head in range(HEADS):
            rows = slice(quarter * QROWS + head * 64, quarter * QROWS + head * 64 + 64)
            qx[rows, :HD] = qf[pl.ds(quarter * QROWS + head, 64, stride=HEADS), :].astype(BF16)
            qx[rows, HD:] = mask

    arrive(0, z * 8 + y * 2 + 1 - h)
    p0_y(start)

    def columns(part):
        def one(dz, carry):
            @pl.when((z >= dz) & ((dz < 3) | (r >= 4)))
            def _():
                arrive(part, me - 8 * dz)
            return carry
        lax.fori_loop(1, 4, one, 0)

    columns(1)
    p1_h(start)
    columns(2)
    p2_y(start)

    def tiles(body, half, count):
        for t in range(count):
            body(pl.multiple_of(half * 1024 + t * TILE, TILE), t)

    ones = jnp.ones((TOK, HD), BF16)

    def diagonal(half, carry):
        def body(base, t):
            rows = pl.ds(base, TILE)
            k = jnp.concatenate([kv[pl.ds(own, TOK), :HD], feat[pl.ds(own, TOK), :]], axis=1)
            v = jnp.concatenate([kv[pl.ds(own, TOK), HD:], ones], axis=1)
            s = lax.dot_general(qx[rows, :], k, (((1,), (1,)), ((), ())), preferred_element_type=F32)
            tok = 128 * half + 64 * (t // 2) + lax.rem(lax.broadcasted_iota(jnp.int32, (TILE, TOK), 0), 64)
            s = jnp.where(lax.broadcasted_iota(jnp.int32, (TILE, TOK), 1) <= tok, s, -BIG)
            m = jnp.broadcast_to(jnp.max(s, axis=1, keepdims=True), (TILE, HD))
            p = jnp.concatenate(
                [jnp.exp2((s[:, j * HD:(j + 1) * HD] - m) * SCALE).astype(BF16) for j in range(TOK // HD)], axis=1)
            mx[rows, :] = m
            acc[rows, :] = jnp.dot(p, v, preferred_element_type=F32)
        tiles(body, half, 4)
        return carry

    lax.fori_loop(0, 2, diagonal, 0)

    def in_plane_p0(n, carry):
        y2 = lax.rem(y + 1 + n // 2, 4)
        arrive(0, z * 8 + y2 * 2 + lax.rem(n, 2))
        return carry

    lax.fori_loop(0, 6, in_plane_p0, 0)
    p0_z(start)

    def pair_p1(dz, carry):
        @pl.when((z >= dz) & ((dz < 3) | (r >= 4)))
        def _():
            arrive(1, (z - dz) * 8 + y * 2 + 1 - h)
        return carry

    lax.fori_loop(0, 4, pair_p1, 0)
    p1_y(start)

    def column_p2(n, carry):
        dz = n // 3
        y1 = lax.rem(y + 1 + lax.rem(n, 3), 4)
        r1 = y1 * 2 + h
        @pl.when((z >= dz) & y_wants(dz, r1, y1, y))
        def _():
            arrive(2, (z - dz) * 8 + r1)
        return carry

    lax.fori_loop(0, 12, column_p2, 0)
    p2_h(start)

    p_copy.wait()
    blk = lax.broadcasted_iota(jnp.int32, (32, 512), 0)
    col = lax.broadcasted_iota(jnp.int32, (32, 512), 1)
    target = jnp.broadcast_to(rrow[...], (32, 512))
    earlier = (jnp.broadcast_to(rcol[...], (32, 512)) == target) & (blk < col // BLOCK)
    rank = jnp.sum(earlier.astype(F32), axis=0, keepdims=True).astype(jnp.int32)
    code = rrow[...] * 32 + rank * BLOCK + lax.rem(col[:1], BLOCK)

    def place(t, carry):
        rows = t * TILE + lax.broadcasted_iota(jnp.int32, (TILE, 512), 0)
        hit = jnp.where(rows == jnp.broadcast_to(code, (TILE, 512)), 1.0, 0.0).astype(BF16)
        outgoing[pl.ds(pl.multiple_of(t * TILE, TILE), TILE), :] = jnp.dot(
            hit, prior[...], preferred_element_type=F32).astype(BF16)
        return carry

    lax.fori_loop(0, 4, place, 0)

    def slot_rows(ref, i):
        return ref.at[pl.ds(pl.multiple_of(i * 32, 32), 32), :]

    def migrate(d):
        there = lax.rem(me + d, N_INST)
        return pltpu.make_async_remote_copy(
            src_ref=slot_rows(outgoing, there), dst_ref=slot_rows(mig_ref, me),
            send_sem=msem.at[d], recv_sem=mrsem.at[d], device_id=(there, hd), device_id_type=MESH)

    stay = pltpu.make_async_copy(slot_rows(outgoing, me), slot_rows(mig_ref, me), loc.at[3])

    def collect(g):
        def one(n, carry):
            src = me - 1 - g * GRP - n
            zs, rs = src // 8, lax.rem(src, 8)
            @pl.when(src >= 0)
            def _():
                @pl.when(zs < z)
                def _():
                    arrive(0, src)
                @pl.when(rs // 2 != y)
                def _():
                    arrive(1, src)
                @pl.when(lax.rem(rs, 2) != h)
                def _():
                    arrive(2, src)
            return carry
        lax.fori_loop(0, GRP, one, 0)

    keys = GRP * TOK
    many = jnp.ones((keys, HD), BF16)

    def attend(g, first_tile, count):
        @pl.when(me - 1 - g * GRP >= 0)
        def _():
            ks = pl.ds(pl.multiple_of((me - g * GRP - GRP + PAD) * TOK, TOK), keys)
            for t in range(count):
                rows = pl.ds(pl.multiple_of(first_tile * TILE + t * TILE, TILE), TILE)
                k = jnp.concatenate([kv[ks, :HD], feat[ks, :]], axis=1)
                s = lax.dot_general(qx[rows, :], k, (((1,), (1,)), ((), ())), preferred_element_type=F32)
                old = mx[rows, :]
                m = jnp.maximum(old, jnp.max(s, axis=1, keepdims=True))
                shrink = jnp.exp2((old - m) * SCALE)
                mx[rows, :] = m
                p = jnp.concatenate(
                    [jnp.exp2((s[:, j * HD:(j + 1) * HD] - m) * SCALE).astype(BF16) for j in range(keys // HD)], axis=1)
                v = jnp.concatenate([kv[ks, HD:], many], axis=1)
                u = jnp.dot(p, v, preferred_element_type=F32)
                a = acc[rows, :]
                acc[rows, :] = jnp.concatenate([a[:, :HD] * shrink, a[:, HD:] * shrink], axis=1) + u

    def full_step(g, carry):
        collect(g)
        attend(g, 0, 8)
        return carry

    lax.fori_loop(0, 3, full_step, 0)

    def go(d, carry):
        migrate(d).start()
        return carry

    stay.start()
    lax.fori_loop(1, N_INST, go, 0)

    def half_step(base):
        def step(g, carry):
            attend(g, base, 4)
            return carry
        return step

    collect(3)
    collect(4)
    lax.fori_loop(3, 5, half_step((1 - xl) * 4), 0)

    def finish(half):
        for which in range(2):
            quarter = half * 2 + (1 - c if which == 0 else c)
            for head in range(HEADS):
                rows = pl.ds(pl.multiple_of(quarter * QROWS + head * 64, 64), 64)
                a = acc[rows, :]
                att[which * 64:(which + 1) * 64, head * HD:(head + 1) * HD] = (a[:, :HD] / a[:, HD:]).astype(BF16)

    def hop(src, dst, n, slot, target):
        return pltpu.make_async_remote_copy(
            src_ref=src.at[n], dst_ref=dst.at[n], send_sem=rs_s.at[slot, n], recv_sem=rs_r.at[slot, n],
            device_id=target, device_id_type=MESH)

    def project(n):
        return jnp.dot(att[...], wbuf[:, pl.ds(pl.multiple_of(n * CW, CW), CW)], preferred_element_type=F32)

    finish(1 - xl)
    w_copy.wait()

    def merge(n):
        hop(s1_out, s1_in, n, 0, sib).wait_recv()
        x_out[n] = (keep[n] + s1_in[n].astype(F32)).astype(BF16)
        hop(x_out, x_in, n, 1, across).start()

    def first_half(n, carry):
        p = project(n)
        s1_out[n] = p[:64].astype(BF16)
        hop(s1_out, s1_in, n, 0, sib).start()
        keep[n] = p[64:]
        @pl.when(n >= 1)
        def _():
            merge(n - 1)
        return carry

    lax.fori_loop(0, CHUNKS, first_half, 0)
    merge(CHUNKS - 1)

    lax.fori_loop(3, 5, half_step(xl * 4), 0)
    finish(xl)

    def second_half(n, carry):
        p = project(n)
        s2_out[n] = p[:64].astype(BF16)
        hop(s2_out, s2_in, n, 2, sib).start()
        keep[n] = p[64:]
        return carry

    lax.fori_loop(0, CHUNKS, second_half, 0)

    def last(n, carry):
        hop(s2_out, s2_in, n, 2, sib).wait_recv()
        hop(x_out, x_in, n, 1, across).wait_recv()
        out_ref[:, pl.ds(pl.multiple_of(n * CW, CW), CW)] = (
            keep[n] + s2_in[n].astype(F32) + x_in[n].astype(F32)).astype(BF16)
        return carry

    lax.fori_loop(0, CHUNKS, last, 0)

    p0_h(done)
    p0_y(done)
    p0_z(done)
    z_first(1, done)
    p1_h(done)
    p1_y(done)
    z_first(2, done)
    p2_y(done)
    p2_h(done)
    stay.wait()

    def gone(d, carry):
        migrate(d).wait()
        return carry

    lax.fori_loop(1, N_INST, gone, 0)

    def sent(n, carry):
        hop(s1_out, s1_in, n, 0, sib).wait_send()
        hop(x_out, x_in, n, 1, across).wait_send()
        hop(s2_out, s2_in, n, 2, sib).wait_send()
        return carry

    lax.fori_loop(0, CHUNKS, sent, 0)


def shards(queries, keys, values, lengths, prior_kv, routes, out_weight):
    rows = TOK * HEADS
    vmem = pl.BlockSpec(memory_space=pltpu.VMEM)
    hbm = pl.BlockSpec(memory_space=pl.ANY)
    blocks = (PAD + N_INST) * TOK
    quarter = (CHUNKS, 64, CW)
    projected, migrated = pl.pallas_call(
        kernel,
        out_shape=(
            jax.ShapeDtypeStruct((64, CHUNKS * CW), BF16),
            jax.ShapeDtypeStruct((N_INST * 2 * BLOCK, 2 * HD), BF16),
        ),
        in_specs=[pl.BlockSpec(memory_space=pltpu.SMEM), hbm, vmem, vmem, hbm, vmem, vmem, hbm],
        out_specs=(vmem, hbm),
        scratch_shapes=[
            pltpu.VMEM((blocks, 2 * HD), BF16),
            pltpu.VMEM((blocks, HD), BF16),
            pltpu.VMEM((rows, HD), BF16),
            pltpu.VMEM((rows, HD), F32),
            pltpu.VMEM((rows, 2 * HD), BF16),
            pltpu.VMEM((rows, 2 * HD), F32),
            pltpu.VMEM((rows, HD), F32),
            pltpu.VMEM((512, 2 * HD), BF16),
            pltpu.VMEM((1024, 2 * HD), BF16),
            pltpu.VMEM((HEADS * HD, CHUNKS * CW), BF16),
            pltpu.VMEM((128, HEADS * HD), BF16),
            pltpu.VMEM(quarter, F32),
            pltpu.VMEM(quarter, BF16),
            pltpu.VMEM(quarter, BF16),
            pltpu.VMEM(quarter, BF16),
            pltpu.VMEM(quarter, BF16),
            pltpu.VMEM(quarter, BF16),
            pltpu.VMEM(quarter, BF16),
            pltpu.SemaphoreType.DMA((4,)),
            pltpu.SemaphoreType.DMA((3, 32)),
            pltpu.SemaphoreType.DMA((3, 32)),
            pltpu.SemaphoreType.DMA((32,)),
            pltpu.SemaphoreType.DMA((32,)),
            pltpu.SemaphoreType.DMA((3, CHUNKS)),
            pltpu.SemaphoreType.DMA((3, CHUNKS)),
        ],
        compiler_params=pltpu.CompilerParams(
            collective_id=0, has_side_effects=True, vmem_limit_bytes=60 * 2 ** 20),
        name="attend_project_migrate",
    )(
        lengths,
        queries.reshape(rows, HD),
        keys.reshape(TOK, HD),
        values.reshape(TOK, HD),
        prior_kv.reshape(512, 2 * HD),
        routes,
        jnp.repeat(routes.reshape(1, 32), BLOCK, axis=1),
        out_weight,
    )
    return projected, migrated.reshape(64, BLOCK, 1, 2 * HD)


def solution(mesh):
    placed = (
        P("inst", "head", None),
        P("inst", "head", None),
        P("inst", "head", None),
        P(),
        P("inst", "head", None),
        P("inst", None),
        P("head", None),
    )
    return jax.shard_map(
        shards,
        mesh=mesh,
        in_specs=placed,
        out_specs=(P(("inst", "head"), None), P("inst", None, "head", None)),
        check_vma=False,
    )
```

time: 226 us -> 71.8 us (0.32)
  waiting for transfers between devices: 100 us -> 0 us
  Pallas kernels: 0 us -> 63.7 us
  matrix products: 57.1 us -> 0 us
  other arithmetic: 27 us -> 0 us
  blocking collectives: 22.4 us -> 0 us
  between operations: 13.9 us -> 0.64 us
  local copies, waits for them, and re-layouts: 2.75 us -> 6.47 us
    all_gather x2 -> x0, waiting for transfers between devices: 89.9 us -> none  [the longest x1 66.7 us: shards(): key_piece = lax.all_gather(keys, 'inst', axis=0, tiled=True)]
    pallas_call x0 -> x1, Pallas kernels: none -> 63.7 us  [shards(): pl.pallas_call(kernel, out_shape=(jax.ShapeDtypeStruct((64, CHUNKS * CW),...]
    dot_general x4 -> x0, matrix products: 57.1 us -> none  [the longest x1 25 us: shards(): jnp.einsum('qcgd,kcd->cgqk', query_grouped, key_piece, preferred_element_...]
    all_to_all x1 -> x0, blocking collectives: 22.4 us -> none  [shards(): lax.all_to_all(outgoing, 'inst', split_axis=0, concat_axis=0, tiled=True)]
    reduce_sum x4 -> x0, other arithmetic: 22.3 us -> none  [the longest x1 21.9 us: shards(): totals = jnp.sum(weights, axis=-1)]
    reduce_scatter x1 -> x0, waiting for transfers between devices: 9.76 us -> none  [shards(): lax.psum_scatter(jnp.dot(attended, out_weight, preferred_element_type=jnp...]
    and x1 -> x0, other arithmetic: 3.73 us -> none  [shards(): (key_pos[None, :] <= query_pos[:, None]) & (key_doc[None, :] == query_doc...]
    unnamed x9 -> x3, local copies, waits for them, and re-layouts: 2.49 us -> 5.08 us
  transfers between devices with their start and end apart: 3 -> 0, of which waited for: 3 -> 0; matrix products, arithmetic and copies ran while one was open for 24% -> 0% of each run, Pallas kernels for 0% -> 0%
where the time goes in v1:
time: 71.8 us; the launch traced here: 70.8 us
  Pallas kernels  63.7 us (89%)
  local copies, waits for them, and re-layouts  6.47 us (9%)
    pallas_call x1, Pallas kernels, shards(): pl.pallas_call(kernel, out_shape=(jax.ShapeDtypeStruct((64, CHUNKS * CW),...  63.7 us
    unnamed x3, local copies, waits for them, and re-layouts  5.08 us

profile of v1, /device:TPU:97, one launch (start us, length us, event | category | flops | bytes accessed | tf_op | source)
XLA Modules:
  0.0 70.8 jit_solution(3422882559550925227)
XLA Ops:
  0.6 0.7 %broadcast_in_dim.5 = s32[32,16]{1,0:T(8,128)S(1)} broadcast(s32[32]{0:T(128)} %bitcast.13), dimensions={0} | broadcast | bytes 2176 | tf_op jit(solution)/shard_map/broadcast_in_dim | solution.py:498
  1.4 0.7 broadcast_in_dim.6.rrow
  2.0 1.3 %copy.11.rcol = s32[32,1]{1,0:T(8,128)} copy(s32[32,1]{0,1:T(1,128)} %param.12) | data formatting | bytes 256 | tf_op args[5]
  3.4 63.7 %attend_project_migrate.1 = (bf16[64,4096]{1,0:T(8,128)(2,1)}, bf16[1024,256]{1,0:T(8,128)(2,1)}) custom-call(s32[4]{0:T(128)} %lengths.1, bf16[2048,128]{1,0:T(8,128)(2,1)} %bitcast.9, bf16[256,128]{1,0:T(8,128)(2,1)} %bitcast.11, bf16[256,128]{1,0:T(8,128)(2,1)} %bitcast.12, bf16[512,256]{1,0:T(8,128)(2,1)} %bitcast.10, s32[32,1]{1,0:T(8,128)} %copy.11.rcol, ...), custom_call_target="tpu_custom_call" | custom-call | tf_op jit(solution)/shard_map/attend_project_migrate/pallas_call | solution.py:453
  67.0 1.9 %copy.15 = bf16[64,4096]{1,0:T(8,128)(2,1)} copy(bf16[64,4096]{1,0:T(8,128)(2,1)} %get-tuple-element.12) | data formatting | bytes 1048576
  68.9 1.9 %copy.16 = bf16[64,16,1,256]{3,1,2,0:T(8,128)(2,1)} copy(bf16[64,16,1,256]{3,1,2,0:T(8,128)(2,1)} %bitcast.8) | data formatting | bytes 1048576

commit v2 on v1

--- a/solution.py
+++ b/solution.py
@@ -34,7 +34,7 @@
     return doc
 
 
-def kernel(lengths, q_hbm, k_ref, v_ref, prior_hbm, rcol, rrow, w_hbm,
+def kernel(lengths, q_hbm, k_ref, v_ref, prior_hbm, routes, w_hbm,
            out_ref, mig_ref,
            kv, feat, qraw, qf, qx, acc, mx, prior, outgoing, wbuf, att,
            keep, s1_out, s1_in, x_out, x_in, s2_out, s2_in,
@@ -82,88 +82,167 @@
     def arrive(part, blk):
         send(part, blk, me, 0).wait_recv()
 
-    def z_first(part, act):
+    def needs(dst, src):
+        return (dst - src >= 1) & (dst - src <= WINDOW)
+
+    def unroll(first, end, body):
+        for n in range(first, end):
+            body(n, 0)
+
+    def wrap(v):
+        return jnp.where(v >= 4, v - 4, v)
+
+    def p0_h(act):
+        act(send(0, me, z * 8 + y * 2 + 1 - h, 0))
+
+    def p0_y(h1, slot, act):
+        def one(n, carry):
+            y2 = wrap(y + 1 + n)
+            @pl.when((z < 3) | (y2 * 2 + h > y * 2 + h1))
+            def _():
+                act(send(0, z * 8 + y * 2 + h1, z * 8 + y2 * 2 + h, slot + n))
+            return carry
+        unroll(0, 3, one)
+
+    def p0_z(r1, slot, act):
+        def one(dz, carry):
+            src, dst = z * 8 + r1, me + 8 * dz
+            @pl.when((z + dz < 4) & needs(dst, src))
+            def _():
+                act(send(0, src, dst, slot + dz))
+            return carry
+        unroll(1, 4, one)
+
+    def p0_rest(dz, act):
+        def one(n, carry):
+            src, dst = z * 8 + wrap(y + 1 + n // 2) * 2 + n % 2, me + 8 * dz
+            @pl.when((z + dz < 4) & needs(dst, src))
+            def _():
+                act(send(0, src, dst, 16 + dz * 6 + n))
+            return carry
+        unroll(0, 6, one)
+
+    def p0_plane():
+        def one(n, carry):
+            r1 = wrap(y + 1 + n // 2) * 2 + n % 2
+            @pl.when((z < 3) | (r > r1))
+            def _():
+                arrive(0, z * 8 + r1)
+            return carry
+        unroll(0, 6, one)
+
+    def column(dz):
+        return (z >= dz) & ((dz < 3) | (r >= 4))
+
+    def p12_z(part, act):
         def one(dz, carry):
             @pl.when((z + dz < 4) & ((dz < 3) | (r >= 4)))
             def _():
                 act(send(part, me, me + 8 * dz, dz - 1))
             return carry
-        lax.fori_loop(1, 4, one, 0)
-
-    def p0_h(act):
-        act(send(0, me, z * 8 + y * 2 + 1 - h, 0))
-
-    def p0_y(act):
-        def one(n, carry):
-            y2 = lax.rem(y + 1 + n // 2, 4)
-            act(send(0, z * 8 + y * 2 + lax.rem(n, 2), z * 8 + y2 * 2 + h, 1 + n))
-            return carry
-        lax.fori_loop(0, 6, one, 0)
-
-    def needs(dst, src):
-        return (dst - src >= 1) & (dst - src <= WINDOW)
-
-    def p0_z(act):
-        def one(n, carry):
-            dz, src = 1 + n // 8, z * 8 + 7 - lax.rem(n, 8)
-            dst = me + 8 * dz
-            @pl.when((z + dz < 4) & needs(dst, src))
-            def _():
-                act(send(0, src, dst, 7 + n))
-            return carry
-        lax.fori_loop(0, 24, one, 0)
-
-    def p1_h(act):
-        def one(dz, carry):
-            @pl.when((z >= dz) & ((dz < 3) | (r >= 4)))
-            def _():
-                act(send(1, me - 8 * dz, z * 8 + y * 2 + 1 - h, 3 + dz))
-            return carry
-        lax.fori_loop(0, 4, one, 0)
-
-    def p1_y(act):
-        def one(n, carry):
-            dz = n // 6
-            y2 = lax.rem(y + 1 + lax.rem(n, 6) // 2, 4)
-            src = (z - dz) * 8 + y * 2 + lax.rem(n, 2)
-            dst = z * 8 + y2 * 2 + h
+        unroll(1, 4, one)
+
+    def p1_h(dz, act):
+        @pl.when(column(dz))
+        def _():
+            act(send(1, me - 8 * dz, z * 8 + y * 2 + 1 - h, 3 + dz))
+
+    def p1_y(dz, h1, slot, act):
+        def one(n, carry):
+            src, dst = (z - dz) * 8 + y * 2 + h1, z * 8 + wrap(y + 1 + n) * 2 + h
             @pl.when((z >= dz) & needs(dst, src))
             def _():
-                act(send(1, src, dst, 7 + n))
-            return carry
-        lax.fori_loop(0, 24, one, 0)
-
-    def y_wants(dz, src_r, src_y, y2):
-        return (((dz == 0) & (y2 > src_y)) | (dz == 1)
-                | ((dz == 2) & (src_r >= 2 * y2 - 4)) | ((dz == 3) & (src_r >= 2 * y2 + 4)))
-
-    def p2_y(act):
-        def one(n, carry):
-            dz = n // 3
-            y2 = lax.rem(y + 1 + lax.rem(n, 3), 4)
-            @pl.when((z >= dz) & y_wants(dz, r, y, y2))
-            def _():
-                act(send(2, me - 8 * dz, z * 8 + y2 * 2 + h, 3 + n))
-            return carry
-        lax.fori_loop(0, 12, one, 0)
-
-    def p2_h(act):
-        def one(n, carry):
-            dz, y1 = n // 4, 3 - lax.rem(n, 4)
-            src = (z - dz) * 8 + y1 * 2 + h
+                act(send(1, src, dst, slot + 6 * dz + n))
+            return carry
+        unroll(0, 3, one)
+
+    def y_wants(dz, r1, y1, y2):
+        if dz == 0:
+            return y2 > y1
+        return (z >= dz) & ((dz == 1) | (r1 >= 2 * y2 + (4 if dz == 3 else -4)))
+
+    def p2_y(dz, act):
+        def one(n, carry):
+            y2 = wrap(y + 1 + n)
+            @pl.when(y_wants(dz, r, y, y2))
+            def _():
+                act(send(2, me - 8 * dz, z * 8 + y2 * 2 + h, 3 + dz * 3 + n))
+            return carry
+        unroll(0, 3, one)
+
+    def p2_h(dz, first, count, slot, act):
+        def one(n, carry):
+            src = (z - dz) * 8 + wrap(y + first + n) * 2 + h
             dst = z * 8 + y * 2 + 1 - h
             @pl.when((z >= dz) & needs(dst, src))
             def _():
-                act(send(2, src, dst, 15 + n))
-            return carry
-        lax.fori_loop(0, 16, one, 0)
+                act(send(2, src, dst, slot + dz * 4 + n))
+            return carry
+        unroll(0, count, one)
+
+    def stage0(act):
+        p0_h(act)
+        p12_z(2, act)
+        p12_z(1, act)
+        p2_y(0, act)
+        p0_y(h, 1, act)
+        p1_h(0, act)
+        p1_y(0, h, 8, act)
+        p2_h(0, 0, 1, 16, act)
+        p0_z(r, 6, act)
+
+    def stage1(act, wait):
+        if wait:
+            arrive(0, z * 8 + y * 2 + 1 - h)
+        p0_y(1 - h, 4, act)
+        p0_z(y * 2 + 1 - h, 9, act)
+        if wait:
+            arrive(1, z * 8 + y * 2 + 1 - h)
+        p1_y(0, 1 - h, 11, act)
+        if wait:
+            from_y(0)
+        p2_h(0, 1, 3, 17, act)
+
+    def from_y(dz):
+        def one(n, carry):
+            y1 = wrap(y + 1 + n)
+            @pl.when(y_wants(dz, y1 * 2 + h, y1, y))
+            def _():
+                arrive(2, (z - dz) * 8 + y1 * 2 + h)
+            return carry
+        unroll(0, 3, one)
+
+    def stage2(dz, act, wait):
+        if wait:
+            @pl.when(column(dz))
+            def _():
+                arrive(2, me - 8 * dz)
+                arrive(1, me - 8 * dz)
+        p2_y(dz, act)
+        p1_h(dz, act)
+        p1_y(dz, h, 8, act)
+        p2_h(dz, 0, 1, 16, act)
+
+    def stage3(act, wait):
+        if wait:
+            p0_plane()
+        for dz in (1, 2, 3):
+            p0_rest(dz, act)
+
+    def stage4(dz, act, wait):
+        if wait:
+            @pl.when(column(dz))
+            def _():
+                arrive(1, (z - dz) * 8 + y * 2 + 1 - h)
+        p1_y(dz, 1 - h, 11, act)
+        if wait:
+            from_y(dz)
+        p2_h(dz, 1, 3, 17, act)
 
     start = lambda copy: copy.start()
     done = lambda copy: copy.wait_send()
 
-    p0_h(start)
-    z_first(1, start)
-    z_first(2, start)
+    stage0(start)
 
     ends = []
     total = jnp.int32(0)
@@ -198,22 +277,6 @@
             rows = slice(quarter * QROWS + head * 64, quarter * QROWS + head * 64 + 64)
             qx[rows, :HD] = qf[pl.ds(quarter * QROWS + head, 64, stride=HEADS), :].astype(BF16)
             qx[rows, HD:] = mask
-
-    arrive(0, z * 8 + y * 2 + 1 - h)
-    p0_y(start)
-
-    def columns(part):
-        def one(dz, carry):
-            @pl.when((z >= dz) & ((dz < 3) | (r >= 4)))
-            def _():
-                arrive(part, me - 8 * dz)
-            return carry
-        lax.fori_loop(1, 4, one, 0)
-
-    columns(1)
-    p1_h(start)
-    columns(2)
-    p2_y(start)
 
     def tiles(body, half, count):
         for t in range(count):
@@ -237,53 +300,6 @@
         tiles(body, half, 4)
         return carry
 
-    lax.fori_loop(0, 2, diagonal, 0)
-
-    def in_plane_p0(n, carry):
-        y2 = lax.rem(y + 1 + n // 2, 4)
-        arrive(0, z * 8 + y2 * 2 + lax.rem(n, 2))
-        return carry
-
-    lax.fori_loop(0, 6, in_plane_p0, 0)
-    p0_z(start)
-
-    def pair_p1(dz, carry):
-        @pl.when((z >= dz) & ((dz < 3) | (r >= 4)))
-        def _():
-            arrive(1, (z - dz) * 8 + y * 2 + 1 - h)
-        return carry
-
-    lax.fori_loop(0, 4, pair_p1, 0)
-    p1_y(start)
-
-    def column_p2(n, carry):
-        dz = n // 3
-        y1 = lax.rem(y + 1 + lax.rem(n, 3), 4)
-        r1 = y1 * 2 + h
-        @pl.when((z >= dz) & y_wants(dz, r1, y1, y))
-        def _():
-            arrive(2, (z - dz) * 8 + r1)
-        return carry
-
-    lax.fori_loop(0, 12, column_p2, 0)
-    p2_h(start)
-
-    p_copy.wait()
-    blk = lax.broadcasted_iota(jnp.int32, (32, 512), 0)
-    col = lax.broadcasted_iota(jnp.int32, (32, 512), 1)
-    target = jnp.broadcast_to(rrow[...], (32, 512))
-    earlier = (jnp.broadcast_to(rcol[...], (32, 512)) == target) & (blk < col // BLOCK)
-    rank = jnp.sum(earlier.astype(F32), axis=0, keepdims=True).astype(jnp.int32)
-    code = rrow[...] * 32 + rank * BLOCK + lax.rem(col[:1], BLOCK)
-
-    def place(t, carry):
-        rows = t * TILE + lax.broadcasted_iota(jnp.int32, (TILE, 512), 0)
-        hit = jnp.where(rows == jnp.broadcast_to(code, (TILE, 512)), 1.0, 0.0).astype(BF16)
-        outgoing[pl.ds(pl.multiple_of(t * TILE, TILE), TILE), :] = jnp.dot(
-            hit, prior[...], preferred_element_type=F32).astype(BF16)
-        return carry
-
-    lax.fori_loop(0, 4, place, 0)
 
     def slot_rows(ref, i):
         return ref.at[pl.ds(pl.multiple_of(i * 32, 32), 32), :]
@@ -299,10 +315,10 @@
     def collect(g):
         def one(n, carry):
             src = me - 1 - g * GRP - n
-            zs, rs = src // 8, lax.rem(src, 8)
+            rs = lax.rem(src, 8)
             @pl.when(src >= 0)
             def _():
-                @pl.when(zs < z)
+                @pl.when(src // 8 < z)
                 def _():
                     arrive(0, src)
                 @pl.when(rs // 2 != y)
@@ -336,29 +352,58 @@
                 a = acc[rows, :]
                 acc[rows, :] = jnp.concatenate([a[:, :HD] * shrink, a[:, HD:] * shrink], axis=1) + u
 
-    def full_step(g, carry):
-        collect(g)
-        attend(g, 0, 8)
-        return carry
-
-    lax.fori_loop(0, 3, full_step, 0)
+    def lay_out():
+        p_copy.wait()
+        row = lax.broadcasted_iota(jnp.int32, (32, 32), 0)
+        lane = lax.broadcasted_iota(jnp.int32, (32, 32), 1)
+        target = jnp.broadcast_to(routes[...], (32, 32))
+        same = jnp.sum(jnp.where(row == lane, target, 0).astype(F32), axis=1, keepdims=True).astype(jnp.int32) == target
+        rank = jnp.sum(jnp.where(same & (row < lane), 1.0, 0.0), axis=0, keepdims=True)
+        slot = (2 * target[:8]).astype(F32) + jnp.broadcast_to(rank, (8, 32))
+        blk = lax.broadcasted_iota(jnp.int32, (32, 512), 0)
+        col = lax.broadcasted_iota(jnp.int32, (32, 512), 1)
+        spread = jnp.where(blk == col // BLOCK, 1.0, 0.0).astype(BF16)
+        slots = jnp.dot(slot.astype(BF16), spread, preferred_element_type=F32)
+        code = (slots[:1].astype(jnp.int32)) * BLOCK + lax.rem(col[:1], BLOCK)
+
+        def place(t, carry):
+            rows = t * TILE + lax.broadcasted_iota(jnp.int32, (TILE, 512), 0)
+            hit = jnp.where(rows == jnp.broadcast_to(code, (TILE, 512)), 1.0, 0.0).astype(BF16)
+            outgoing[pl.ds(pl.multiple_of(t * TILE, TILE), TILE), :] = jnp.dot(
+                hit, prior[...], preferred_element_type=F32).astype(BF16)
+            return carry
+
+        lax.fori_loop(0, 4, place, 0)
 
     def go(d, carry):
         migrate(d).start()
         return carry
 
+    stage1(start, True)
+    stage2(1, start, True)
+    stage2(2, start, True)
+    p0_plane()
+    p0_rest(1, start)
+    p0_rest(2, start)
+    stage2(3, start, True)
+    p0_rest(3, start)
+    stage4(1, start, True)
+    lax.fori_loop(0, 2, diagonal, 0)
+    stage4(2, start, True)
+    stage4(3, start, True)
+    collect(0)
+    attend(0, 0, 8)
+    lay_out()
+    collect(1)
+    attend(1, 0, 8)
     stay.start()
     lax.fori_loop(1, N_INST, go, 0)
-
-    def half_step(base):
-        def step(g, carry):
-            attend(g, base, 4)
-            return carry
-        return step
-
+    collect(2)
+    attend(2, (1 - xl) * 4, 4)
     collect(3)
+    attend(3, (1 - xl) * 4, 4)
     collect(4)
-    lax.fori_loop(3, 5, half_step((1 - xl) * 4), 0)
+    attend(4, (1 - xl) * 4, 4)
 
     def finish(half):
         for which in range(2):
@@ -397,7 +442,10 @@
     lax.fori_loop(0, CHUNKS, first_half, 0)
     merge(CHUNKS - 1)
 
-    lax.fori_loop(3, 5, half_step(xl * 4), 0)
+    attend(2, xl * 4, 4)
+    attend(3, xl * 4, 4)
+    attend(4, xl * 4, 4)
+
     finish(xl)
 
     def second_half(n, carry):
@@ -409,6 +457,20 @@
 
     lax.fori_loop(0, CHUNKS, second_half, 0)
 
+    stage0(done)
+    stage1(done, False)
+    stage3(done, False)
+    for dz in (1, 2, 3):
+        stage2(dz, done, False)
+        stage4(dz, done, False)
+    stay.wait()
+
+    def gone(d, carry):
+        migrate(d).wait()
+        return carry
+
+    lax.fori_loop(1, N_INST, gone, 0)
+
     def last(n, carry):
         hop(s2_out, s2_in, n, 2, sib).wait_recv()
         hop(x_out, x_in, n, 1, across).wait_recv()
@@ -418,23 +480,6 @@
 
     lax.fori_loop(0, CHUNKS, last, 0)
 
-    p0_h(done)
-    p0_y(done)
-    p0_z(done)
-    z_first(1, done)
-    p1_h(done)
-    p1_y(done)
-    z_first(2, done)
-    p2_y(done)
-    p2_h(done)
-    stay.wait()
-
-    def gone(d, carry):
-        migrate(d).wait()
-        return carry
-
-    lax.fori_loop(1, N_INST, gone, 0)
-
     def sent(n, carry):
         hop(s1_out, s1_in, n, 0, sib).wait_send()
         hop(x_out, x_in, n, 1, across).wait_send()
@@ -442,6 +487,15 @@
         return carry
 
     lax.fori_loop(0, CHUNKS, sent, 0)
+
+
+def hand_over(a, b, a_out, b_out, sem):
+    first = pltpu.make_async_copy(a, a_out, sem.at[0])
+    second = pltpu.make_async_copy(b, b_out, sem.at[1])
+    first.start()
+    second.start()
+    first.wait()
+    second.wait()
 
 
 def shards(queries, keys, values, lengths, prior_kv, routes, out_weight):
@@ -456,7 +510,7 @@
             jax.ShapeDtypeStruct((64, CHUNKS * CW), BF16),
             jax.ShapeDtypeStruct((N_INST * 2 * BLOCK, 2 * HD), BF16),
         ),
-        in_specs=[pl.BlockSpec(memory_space=pltpu.SMEM), hbm, vmem, vmem, hbm, vmem, vmem, hbm],
+        in_specs=[pl.BlockSpec(memory_space=pltpu.SMEM), hbm, vmem, vmem, hbm, vmem, hbm],
         out_specs=(vmem, hbm),
         scratch_shapes=[
             pltpu.VMEM((blocks, 2 * HD), BF16),
@@ -478,8 +532,8 @@
             pltpu.VMEM(quarter, BF16),
             pltpu.VMEM(quarter, BF16),
             pltpu.SemaphoreType.DMA((4,)),
-            pltpu.SemaphoreType.DMA((3, 32)),
-            pltpu.SemaphoreType.DMA((3, 32)),
+            pltpu.SemaphoreType.DMA((3, 48)),
+            pltpu.SemaphoreType.DMA((3, 48)),
             pltpu.SemaphoreType.DMA((32,)),
             pltpu.SemaphoreType.DMA((32,)),
             pltpu.SemaphoreType.DMA((3, CHUNKS)),
@@ -494,10 +548,20 @@
         keys.reshape(TOK, HD),
         values.reshape(TOK, HD),
         prior_kv.reshape(512, 2 * HD),
-        routes,
-        jnp.repeat(routes.reshape(1, 32), BLOCK, axis=1),
+        routes.reshape(1, 32),
         out_weight,
     )
+    projected, migrated = pl.pallas_call(
+        hand_over,
+        out_shape=(
+            jax.ShapeDtypeStruct(projected.shape, BF16),
+            jax.ShapeDtypeStruct(migrated.shape, BF16),
+        ),
+        in_specs=[vmem, vmem],
+        out_specs=(hbm, hbm),
+        scratch_shapes=[pltpu.SemaphoreType.DMA((2,))],
+        name="hand_over",
+    )(projected, migrated)
     return projected, migrated.reshape(64, BLOCK, 1, 2 * HD)
 
 

time: 71.8 us -> 65 us (0.905)
  local copies, waits for them, and re-layouts: 6.47 us -> 0 us
    unnamed x3 -> x0, local copies, waits for them, and re-layouts: 5.08 us -> none
    pallas_call x0 -> x1, Pallas kernels: none -> 2.18 us  [shards(): pl.pallas_call(hand_over, out_shape=(jax.ShapeDtypeStruct(projected.shape...]
    pallas_call x1, Pallas kernels: 63.7 us -> 61.5 us  [shards(): pl.pallas_call(kernel, out_shape=(jax.ShapeDtypeStruct((64, CHUNKS * CW),...]
    broadcast_in_dim x2 -> x0, local copies, waits for them, and re-layouts: 1.39 us -> none  [shards(): jnp.repeat(routes.reshape(1, 32), BLOCK, axis=1)]
where the time goes in v2:
time: 65 us; the launch traced here: 64.5 us
  Pallas kernels  63.7 us (98%)
  between operations  0.8 us (1%)
    pallas_call x1, Pallas kernels, shards(): pl.pallas_call(kernel, out_shape=(jax.ShapeDtypeStruct((64, CHUNKS * CW),...  61.5 us
    pallas_call x1, Pallas kernels, shards(): pl.pallas_call(hand_over, out_shape=(jax.ShapeDtypeStruct(projected.shape...  2.18 us

profile of v2, /device:TPU:97, one launch (start us, length us, event | category | flops | bytes accessed | tf_op | source)
XLA Modules:
  0.0 64.5 jit_solution(5129786054638848888)
XLA Ops:
  0.6 61.5 %attend_project_migrate.1 = (bf16[64,4096]{1,0:T(8,128)(2,1)}, bf16[1024,256]{1,0:T(8,128)(2,1)}) custom-call(s32[4]{0:T(128)} %lengths.1, bf16[2048,128]{1,0:T(8,128)(2,1)} %bitcast.8, bf16[256,128]{1,0:T(8,128)(2,1)} %bitcast.10, bf16[256,128]{1,0:T(8,128)(2,1)} %bitcast.11, bf16[512,256]{1,0:T(8,128)(2,1)} %bitcast.9, s32[1,32]{1,0:T(1,128)} %bitcast.12, ...), custom_call_target="tpu_custom_call" | custom-call | tf_op jit(solution)/shard_map/attend_project_migrate/pallas_call | solution.py:507
  62.1 2.2 %hand_over.1 = (bf16[64,4096]{1,0:T(8,128)(2,1)}, bf16[1024,256]{1,0:T(8,128)(2,1)}) custom-call(bf16[64,4096]{1,0:T(8,128)(2,1)} %get-tuple-element.6.a, bf16[1024,256]{1,0:T(8,128)(2,1)} %get-tuple-element.7.b), custom_call_target="tpu_custom_call" | custom-call | tf_op jit(solution)/shard_map/hand_over/pallas_call | solution.py:554

commit v3 on v2

--- a/solution.py
+++ b/solution.py
@@ -18,7 +18,7 @@
 WINDOW = 20
 GRP = 4
 PAD = 4
-PARTS = ((0, 96), (96, 48), (144, 112))
+PARTS = ((0, 96), (96, 64), (160, 96))
 QROWS = 512
 TILE = 256
 CHUNKS = 4
@@ -85,24 +85,17 @@
     def needs(dst, src):
         return (dst - src >= 1) & (dst - src <= WINDOW)
 
-    def unroll(first, end, body):
-        for n in range(first, end):
-            body(n, 0)
-
-    def wrap(v):
-        return jnp.where(v >= 4, v - 4, v)
-
     def p0_h(act):
         act(send(0, me, z * 8 + y * 2 + 1 - h, 0))
 
     def p0_y(h1, slot, act):
         def one(n, carry):
-            y2 = wrap(y + 1 + n)
+            y2 = lax.rem(y + 1 + n, 4)
             @pl.when((z < 3) | (y2 * 2 + h > y * 2 + h1))
             def _():
                 act(send(0, z * 8 + y * 2 + h1, z * 8 + y2 * 2 + h, slot + n))
             return carry
-        unroll(0, 3, one)
+        lax.fori_loop(0, 3, one, 0)
 
     def p0_z(r1, slot, act):
         def one(dz, carry):
@@ -111,25 +104,25 @@
             def _():
                 act(send(0, src, dst, slot + dz))
             return carry
-        unroll(1, 4, one)
+        lax.fori_loop(1, 4, one, 0)
 
     def p0_rest(dz, act):
         def one(n, carry):
-            src, dst = z * 8 + wrap(y + 1 + n // 2) * 2 + n % 2, me + 8 * dz
+            src, dst = z * 8 + lax.rem(y + 1 + n // 2, 4) * 2 + lax.rem(n, 2), me + 8 * dz
             @pl.when((z + dz < 4) & needs(dst, src))
             def _():
                 act(send(0, src, dst, 16 + dz * 6 + n))
             return carry
-        unroll(0, 6, one)
+        lax.fori_loop(0, 6, one, 0)
 
     def p0_plane():
         def one(n, carry):
-            r1 = wrap(y + 1 + n // 2) * 2 + n % 2
+            r1 = lax.rem(y + 1 + n // 2, 4) * 2 + lax.rem(n, 2)
             @pl.when((z < 3) | (r > r1))
             def _():
                 arrive(0, z * 8 + r1)
             return carry
-        unroll(0, 6, one)
+        lax.fori_loop(0, 6, one, 0)
 
     def column(dz):
         return (z >= dz) & ((dz < 3) | (r >= 4))
@@ -140,7 +133,7 @@
             def _():
                 act(send(part, me, me + 8 * dz, dz - 1))
             return carry
-        unroll(1, 4, one)
+        lax.fori_loop(1, 4, one, 0)
 
     def p1_h(dz, act):
         @pl.when(column(dz))
@@ -149,12 +142,12 @@
 
     def p1_y(dz, h1, slot, act):
         def one(n, carry):
-            src, dst = (z - dz) * 8 + y * 2 + h1, z * 8 + wrap(y + 1 + n) * 2 + h
+            src, dst = (z - dz) * 8 + y * 2 + h1, z * 8 + lax.rem(y + 1 + n, 4) * 2 + h
             @pl.when((z >= dz) & needs(dst, src))
             def _():
                 act(send(1, src, dst, slot + 6 * dz + n))
             return carry
-        unroll(0, 3, one)
+        lax.fori_loop(0, 3, one, 0)
 
     def y_wants(dz, r1, y1, y2):
         if dz == 0:
@@ -163,22 +156,22 @@
 
     def p2_y(dz, act):
         def one(n, carry):
-            y2 = wrap(y + 1 + n)
+            y2 = lax.rem(y + 1 + n, 4)
             @pl.when(y_wants(dz, r, y, y2))
             def _():
                 act(send(2, me - 8 * dz, z * 8 + y2 * 2 + h, 3 + dz * 3 + n))
             return carry
-        unroll(0, 3, one)
+        lax.fori_loop(0, 3, one, 0)
 
     def p2_h(dz, first, count, slot, act):
         def one(n, carry):
-            src = (z - dz) * 8 + wrap(y + first + n) * 2 + h
+            src = (z - dz) * 8 + lax.rem(y + first + n, 4) * 2 + h
             dst = z * 8 + y * 2 + 1 - h
             @pl.when((z >= dz) & needs(dst, src))
             def _():
                 act(send(2, src, dst, slot + dz * 4 + n))
             return carry
-        unroll(0, count, one)
+        lax.fori_loop(0, count, one, 0)
 
     def stage0(act):
         p0_h(act)
@@ -205,12 +198,12 @@
 
     def from_y(dz):
         def one(n, carry):
-            y1 = wrap(y + 1 + n)
+            y1 = lax.rem(y + 1 + n, 4)
             @pl.when(y_wants(dz, y1 * 2 + h, y1, y))
             def _():
                 arrive(2, (z - dz) * 8 + y1 * 2 + h)
             return carry
-        unroll(0, 3, one)
+        lax.fori_loop(0, 3, one, 0)
 
     def stage2(dz, act, wait):
         if wait:
@@ -352,6 +345,20 @@
                 a = acc[rows, :]
                 acc[rows, :] = jnp.concatenate([a[:, :HD] * shrink, a[:, HD:] * shrink], axis=1) + u
 
+    def full_loop(g, carry):
+        collect(g)
+        attend(g, 0, 8)
+        return carry
+
+    def first_loop(g, carry):
+        collect(g)
+        attend(g, (1 - xl) * 4, 4)
+        return carry
+
+    def second_loop(g, carry):
+        attend(g, xl * 4, 4)
+        return carry
+
     def lay_out():
         p_copy.wait()
         row = lax.broadcasted_iota(jnp.int32, (32, 32), 0)
@@ -389,21 +396,13 @@
     p0_rest(3, start)
     stage4(1, start, True)
     lax.fori_loop(0, 2, diagonal, 0)
+    lay_out()
     stage4(2, start, True)
     stage4(3, start, True)
-    collect(0)
-    attend(0, 0, 8)
-    lay_out()
-    collect(1)
-    attend(1, 0, 8)
+    lax.fori_loop(0, 2, full_loop, 0)
     stay.start()
     lax.fori_loop(1, N_INST, go, 0)
-    collect(2)
-    attend(2, (1 - xl) * 4, 4)
-    collect(3)
-    attend(3, (1 - xl) * 4, 4)
-    collect(4)
-    attend(4, (1 - xl) * 4, 4)
+    lax.fori_loop(2, 5, first_loop, 0)
 
     def finish(half):
         for which in range(2):
@@ -442,9 +441,7 @@
     lax.fori_loop(0, CHUNKS, first_half, 0)
     merge(CHUNKS - 1)
 
-    attend(2, xl * 4, 4)
-    attend(3, xl * 4, 4)
-    attend(4, xl * 4, 4)
+    lax.fori_loop(2, 5, second_loop, 0)
 
     finish(xl)
 

time: 65 us -> 63.3 us (0.974)
  Pallas kernels: 63.7 us -> 62.5 us
    pallas_call x1, Pallas kernels: 61.5 us -> 60.3 us  [shards(): pl.pallas_call(kernel, out_shape=(jax.ShapeDtypeStruct((64, CHUNKS * CW),...]
where the time goes in v3:
time: 63.3 us; the launch traced here: 63.1 us
  Pallas kernels  62.5 us (99%)
  between operations  0.64 us (1%)
    pallas_call x1, Pallas kernels, shards(): pl.pallas_call(kernel, out_shape=(jax.ShapeDtypeStruct((64, CHUNKS * CW),...  60.3 us
    pallas_call x1, Pallas kernels, shards(): pl.pallas_call(hand_over, out_shape=(jax.ShapeDtypeStruct(projected.shape...  2.18 us

profile of v3, /device:TPU:97, one launch (start us, length us, event | category | flops | bytes accessed | tf_op | source)
XLA Modules:
  0.0 63.1 jit_solution(8115505062752802673)
XLA Ops:
  0.6 60.3 %attend_project_migrate.1 = (bf16[64,4096]{1,0:T(8,128)(2,1)}, bf16[1024,256]{1,0:T(8,128)(2,1)}) custom-call(s32[4]{0:T(128)} %lengths.1, bf16[2048,128]{1,0:T(8,128)(2,1)} %bitcast.8, bf16[256,128]{1,0:T(8,128)(2,1)} %bitcast.10, bf16[256,128]{1,0:T(8,128)(2,1)} %bitcast.11, bf16[512,256]{1,0:T(8,128)(2,1)} %bitcast.9, s32[1,32]{1,0:T(1,128)} %bitcast.12, ...), custom_call_target="tpu_custom_call" | custom-call | tf_op jit(solution)/shard_map/attend_project_migrate/pallas_call | solution.py:504
  60.9 2.2 %hand_over.1 = (bf16[64,4096]{1,0:T(8,128)(2,1)}, bf16[1024,256]{1,0:T(8,128)(2,1)}) custom-call(bf16[64,4096]{1,0:T(8,128)(2,1)} %get-tuple-element.6.a, bf16[1024,256]{1,0:T(8,128)(2,1)} %get-tuple-element.7.b), custom_call_target="tpu_custom_call" | custom-call | tf_op jit(solution)/shard_map/hand_over/pallas_call | solution.py:551

commit v4 on v3

--- a/solution.py
+++ b/solution.py
@@ -22,6 +22,7 @@
 QROWS = 512
 TILE = 256
 CHUNKS = 4
+PIECES = 4
 CW = 1024
 BIG = float(2 ** 30)
 SCALE = math.log2(math.e) / math.sqrt(HD)
@@ -391,12 +392,12 @@
     stage2(2, start, True)
     p0_plane()
     p0_rest(1, start)
+    stage2(3, start, True)
+    stage4(1, start, True)
     p0_rest(2, start)
-    stage2(3, start, True)
-    p0_rest(3, start)
-    stage4(1, start, True)
     lax.fori_loop(0, 2, diagonal, 0)
     lay_out()
+    p0_rest(3, start)
     stage4(2, start, True)
     stage4(3, start, True)
     lax.fori_loop(0, 2, full_loop, 0)
@@ -486,13 +487,22 @@
     lax.fori_loop(0, CHUNKS, sent, 0)
 
 
-def hand_over(a, b, a_out, b_out, sem):
-    first = pltpu.make_async_copy(a, a_out, sem.at[0])
-    second = pltpu.make_async_copy(b, b_out, sem.at[1])
-    first.start()
-    second.start()
-    first.wait()
-    second.wait()
+def hand_over(a, b, a_out, b_out, a_here, b_here, arrived, left):
+    moves = []
+    for i, (src, here, dst) in enumerate(((a, a_here, a_out), (b, b_here, b_out))):
+        rows = src.shape[0] // PIECES
+        for n in range(PIECES):
+            part = pl.ds(n * rows, rows)
+            moves.append((
+                pltpu.make_async_copy(src.at[part, :], here.at[part, :], arrived.at[i, n]),
+                pltpu.make_async_copy(here.at[part, :], dst.at[part, :], left.at[i, n])))
+    for inward, _ in moves:
+        inward.start()
+    for inward, outward in moves:
+        inward.wait()
+        outward.start()
+    for _, outward in moves:
+        outward.wait()
 
 
 def shards(queries, keys, values, lengths, prior_kv, routes, out_weight):
@@ -554,9 +564,14 @@
             jax.ShapeDtypeStruct(projected.shape, BF16),
             jax.ShapeDtypeStruct(migrated.shape, BF16),
         ),
-        in_specs=[vmem, vmem],
+        in_specs=[hbm, hbm],
         out_specs=(hbm, hbm),
-        scratch_shapes=[pltpu.SemaphoreType.DMA((2,))],
+        scratch_shapes=[
+            pltpu.VMEM(projected.shape, BF16),
+            pltpu.VMEM(migrated.shape, BF16),
+            pltpu.SemaphoreType.DMA((2, PIECES)),
+            pltpu.SemaphoreType.DMA((2, PIECES)),
+        ],
         name="hand_over",
     )(projected, migrated)
     return projected, migrated.reshape(64, BLOCK, 1, 2 * HD)

time: 63.3 us -> 63.1 us (level)
  no operation moved by 1% of the time
where the time goes in v4:
time: 63.1 us; the launch traced here: 62.9 us
  Pallas kernels  62.3 us (99%)
  between operations  0.64 us (1%)
    pallas_call x1, Pallas kernels, shards(): pl.pallas_call(kernel, out_shape=(jax.ShapeDtypeStruct((64, CHUNKS * CW),...  60.2 us
    pallas_call x1, Pallas kernels, shards(): pl.pallas_call(hand_over, out_shape=(jax.ShapeDtypeStruct(projected.shape...  2.09 us

profile of v4, /device:TPU:97, one launch (start us, length us, event | category | flops | bytes accessed | tf_op | source)
XLA Modules:
  0.0 62.9 jit_solution(1323659314354423916)
XLA Ops:
  0.6 60.2 %attend_project_migrate.1 = (bf16[64,4096]{1,0:T(8,128)(2,1)}, bf16[1024,256]{1,0:T(8,128)(2,1)}) custom-call(s32[4]{0:T(128)} %lengths.1, bf16[2048,128]{1,0:T(8,128)(2,1)} %bitcast.8, bf16[256,128]{1,0:T(8,128)(2,1)} %bitcast.10, bf16[256,128]{1,0:T(8,128)(2,1)} %bitcast.11, bf16[512,256]{1,0:T(8,128)(2,1)} %bitcast.9, s32[1,32]{1,0:T(1,128)} %bitcast.12, ...), custom_call_target="tpu_custom_call" | custom-call | tf_op jit(solution)/shard_map/attend_project_migrate/pallas_call | solution.py:514
  60.8 2.1 %hand_over.1 = (bf16[64,4096]{1,0:T(8,128)(2,1)}, bf16[1024,256]{1,0:T(8,128)(2,1)}) custom-call(bf16[64,4096]{1,0:T(8,128)(2,1)} %get-tuple-element.6.a, bf16[1024,256]{1,0:T(8,128)(2,1)} %get-tuple-element.7.b), custom_call_target="tpu_custom_call" | custom-call | tf_op jit(solution)/shard_map/hand_over/pallas_call | solution.py:561
